TPU v7x, 32 devices: a whole 2x2x4 slice. The times are simulated.
32 devices in a mesh: gx: 8 (over z, x), gy: 2 (over core), gz: 2 (over y).
Axes of the slice: x: 2, y: 2, z: 4, core: 2. Of those that a mesh axis runs over, the one named last changes fastest.
Arguments:
- bands: float32 [4, 96, 96, 256], P(None, 'gx', 'gy', 'gz'), may hold values from -6 to 6
- stencil_coef: float32 [27], replicated, may hold values from -0.12 to 0.12
Outputs:
- basis: float32 [4, 96, 96, 256], P(None, 'gx', 'gy', 'gz')
- ritz: float32 [4, 4], replicated
All inputs are finite; a program needn't handle non-finite values.
Results may differ from a plain program's by a relative error of at most 0.000071.
Values sent between devices are 32-bit elements; how exact they have to be, the bound alone decides.
A program may use at most 64 MiB of HBM per device.

v0:
```python
import functools

import jax
import jax.numpy as jnp
from jax import lax
from jax.experimental import pallas as pl
from jax.experimental.pallas import tpu as pltpu
from jax.sharding import PartitionSpec as P

DEGREE = 4

lower_edge = 1.0
upper_edge = 6.5
HALF = (upper_edge - lower_edge) / 2
CENTER = (upper_edge + lower_edge) / 2

MESH = pl.DeviceIdType.MESH
NS = DEGREE + 1
LANES = 128
F32 = jnp.float32


def square(position, total):
    scaled = jnp.minimum(position, total - position).astype(F32) / (0.5 * total)
    return scaled * scaled


def kernel(
    sizes, shape, bands_ref, coef_ref, basis_ref, ritz_ref,
    cur, zm, zp, kin, packed, arrived, xrecv, ysend, yrecv, csend, crecv,
    sum_x, sum_yz,
    load_sem, zs_sem, zr_sem, xs_sem, xr_sem, ys_sem, yr_sem, cs_sem, cr_sem,
    ax_s, ax_r, ay_s, ay_r,
):
    nx, ny, nz = sizes
    nb, cx, cy, cz = shape
    rows = cy + 8
    wide = nb + 1
    gx, gy, gz = lax.axis_index("gx"), lax.axis_index("gy"), lax.axis_index("gz")

    def dev(dx, dy, dz):
        return (lax.rem(gx + dx + nx, nx), lax.rem(gy + dy + ny, ny), lax.rem(gz + dz + nz, nz))

    load = pltpu.make_async_copy(bands_ref, cur.at[0, 0:nb, 1 : cx + 1, 0:cy], load_sem)
    load.start()

    barrier = pltpu.get_barrier_semaphore()
    greeted = [dev(k, 0, 0) for k in range(1, nx)]
    others = [(j, k) for j in range(ny) for k in range(nz) if (j, k) != (0, 0)]
    greeted += [dev(0, j, k) for j, k in others]
    greeted += [dev(dx, dy, 0) for dx in (-1, 1) for dy in (-1, 1)]
    for target in greeted:
        pl.semaphore_signal(barrier, inc=1, device_id=target, device_id_type=MESH)

    lane = lax.broadcasted_iota(jnp.int32, (cy, LANES), 1)
    row = lax.broadcasted_iota(jnp.int32, (cy, LANES), 0)
    group = lax.rem(lane, 32)
    fy = square(row + gy * cy, ny * cy)
    kin[0] = fy + square(lane + gz * cz, nz * cz)
    strip_z = gz * cz + jnp.where(group < 16, group - 8, group + (cz - 24)) + nz * cz
    kin[1] = fy + square(lax.rem(strip_z, nz * cz), nz * cz)

    load.wait()

    half_rows = cy // 2

    def pick_strip(plane):
        result = jnp.zeros((cy, LANES), F32)
        for b in range(nb):
            v = cur[0, b, plane, 0:cy, :]
            left = pltpu.roll(v, (32 * b + 8) % LANES, 1)
            right = pltpu.roll(v, (32 * b + 24) % LANES, 1)
            mine = jnp.where(group < 16, left, right)
            result = jnp.where(lane // 32 == b, mine, result)
        return result

    outer = (group < 8) | (group >= 24)
    outer_half = outer[0:half_rows]

    @pl.loop(0, cx)
    def _(i):
        own = pick_strip(i + 1)
        cur[0, nb, i + 1, 0:cy, :] = own
        packed[i] = jnp.where(
            outer_half, own[0:half_rows], pltpu.roll(own[half_rows:cy], 16, 1)
        )

    pl.semaphore_wait(barrier, len(greeted))

    z_copy = pltpu.make_async_remote_copy(
        src_ref=packed, dst_ref=arrived, send_sem=zs_sem, recv_sem=zr_sem,
        device_id=dev(0, 0, 1), device_id_type=MESH,
    )
    z_copy.start()
    z_copy.wait()

    @pl.loop(0, cx)
    def _(i):
        there = arrived[i]
        own = cur[0, nb, i + 1, 0:cy, :]
        full = jnp.concatenate([there, pltpu.roll(there, LANES - 16, 1)], axis=0)
        cur[0, nb, i + 1, 0:cy, :] = jnp.where(outer, full, own)

    def start_sends(step):
        now = step % 2
        copies = []

        @pl.loop(0, wide)
        def _(b):
            for p in range(1, cx + 1):
                ysend[step, 0, b, p : p + 1, :] = cur[now, b, p, 0:1, :]
                ysend[step, 1, b, p : p + 1, :] = cur[now, b, p, cy - 1 : cy, :]
            for i, p in enumerate((1, cx)):
                for j, r in enumerate((0, cy - 1)):
                    csend[step, i, j, pl.ds(b, 1), :] = cur[now, b, p, r : r + 1, :]

        for i, p in enumerate((1, cx)):
            copies.append(pltpu.make_async_remote_copy(
                src_ref=cur.at[now, :, p, 0:cy], dst_ref=xrecv.at[step, i],
                send_sem=xs_sem.at[step, i], recv_sem=xr_sem.at[step, i],
                device_id=dev(2 * i - 1, 0, 0), device_id_type=MESH,
            ))
        for j in range(2):
            copies.append(pltpu.make_async_remote_copy(
                src_ref=ysend.at[step, j], dst_ref=yrecv.at[step, j],
                send_sem=ys_sem.at[step, j], recv_sem=yr_sem.at[step, j],
                device_id=dev(0, 2 * j - 1, 0), device_id_type=MESH,
            ))
        for i in range(2):
            for j in range(2):
                copies.append(pltpu.make_async_remote_copy(
                    src_ref=csend.at[step, i, j], dst_ref=crecv.at[step, i, j],
                    send_sem=cs_sem.at[step, 2 * i + j], recv_sem=cr_sem.at[step, 2 * i + j],
                    device_id=dev(2 * i - 1, 2 * j - 1, 0), device_id_type=MESH,
                ))
        for copy in copies:
            copy.start()
        return copies

    def shift_z(now, plane, first, count):
        part = pl.ds(first, count)
        at = lax.broadcasted_iota(jnp.int32, (count, LANES), 1)
        strip = cur[now, nb, plane, part, :]
        zm[nb, plane, part, :] = pltpu.roll(strip, 1, 1)
        zp[nb, plane, part, :] = pltpu.roll(strip, LANES - 1, 1)
        for b in range(nb):
            v = cur[now, b, plane, part, :]
            before = pltpu.roll(strip, (LANES - 32 * b - 7) % LANES, 1)
            after = pltpu.roll(strip, (LANES - 1 - 32 * b - 24) % LANES, 1)
            zm[b, plane, part, :] = jnp.where(at == 0, before, pltpu.roll(v, 1, 1))
            zp[b, plane, part, :] = jnp.where(at == LANES - 1, after, pltpu.roll(v, LANES - 1, 1))

    def apply_plane(step, b, plane):
        now, later = step % 2, 1 - step % 2
        fields = (zm, cur.at[now], zp)
        sums = []
        for y in range(3):
            total = None
            for x in range(3):
                for z in range(3):
                    c = coef_ref[9 * x + 3 * y + z]
                    span = pl.ds(0, cy) if y == 1 else pl.ds(0, rows)
                    term = c * fields[z][b, plane + (x - 1), span, :]
                    total = term if total is None else total + term
            sums.append(total)
        v = cur[now, b, plane, 0:cy, :]
        scale = 1.0 / HALF if step == 0 else (2.0 / HALF if step < DEGREE else 1.0)
        fx = square(gx * cx + plane - 1, nx * cx)
        if step < DEGREE:
            fx = fx - CENTER
        total = sums[1] + pltpu.roll(sums[0], 1, 0)[0:cy] + pltpu.roll(sums[2], rows - 1, 0)[0:cy]
        total = (total + (kin[b // nb] + fx) * v) * scale
        if 0 < step < DEGREE:
            total = total - cur[later, b, plane, 0:cy, :]
        cur[later, b, plane, 0:cy, :] = total

    gram_pairs = [(p, q) for p in range(nb) for q in range(p + 1)]
    pairs = [(p, q) for p in range(nb) for q in range(nb)]
    fslot, hslot = DEGREE % 2, 1 - DEGREE % 2

    def fold(a):
        total = a[0:8]
        for k in range(8, cy, 8):
            total = total + a[k : k + 8]
        return total

    copies = start_sends(0)
    for step in range(NS):
        now = step % 2
        live = wide if step < DEGREE else nb
        x_copies, y_copies, c_copies = copies[0:2], copies[2:4], copies[4:8]

        @pl.loop(1, cx + 1)
        def _(p):
            shift_z(now, p, 0, cy)

        if step == DEGREE:
            def gram_plane(p, acc):
                f = [cur[fslot, b, p + 1, 0:cy, :] for b in range(nb)]
                return tuple(a + fold(f[i] * f[j]) for a, (i, j) in zip(acc, gram_pairs))

            grams = lax.fori_loop(
                0, cx, gram_plane, tuple(jnp.zeros((8, LANES), F32) for _ in gram_pairs)
            )

        for copy in y_copies:
            copy.wait_recv()

        @pl.loop(0, wide)
        def _(b):
            for p in range(1, cx + 1):
                cur[now, b, p, cy : cy + 1, :] = yrecv[step, 0, b, p : p + 1, :]
                cur[now, b, p, rows - 1 : rows, :] = yrecv[step, 1, b, p : p + 1, :]

        @pl.loop(1, cx + 1)
        def _(p):
            shift_z(now, p, cy, 8)

        @pl.loop(0, live * (cx - 2))
        def _(t):
            apply_plane(step, t // (cx - 2), lax.rem(t, cx - 2) + 2)

        for copy in x_copies + c_copies:
            copy.wait_recv()

        @pl.loop(0, wide)
        def _(b):
            for i, p in enumerate((cx + 1, 0)):
                cur[now, b, p, 0:cy, :] = xrecv[step, i, b]
                cur[now, b, p, cy : cy + 1, :] = crecv[step, i, 0, pl.ds(b, 1), :]
                cur[now, b, p, rows - 1 : rows, :] = crecv[step, i, 1, pl.ds(b, 1), :]

        for p in (0, cx + 1):
            shift_z(now, p, 0, rows)

        @pl.loop(0, live)
        def _(b):
            apply_plane(step, b, 1)
            apply_plane(step, b, cx)

        for copy in copies:
            copy.wait_send()
        if step < DEGREE:
            copies = start_sends(step + 1)

    def dot_plane(p, acc):
        f = [cur[fslot, b, p + 1, 0:cy, :] for b in range(nb)]
        h = [cur[hslot, b, p + 1, 0:cy, :] for b in range(nb)]
        return tuple(a + fold(f[i] * h[j]) for a, (i, j) in zip(acc, pairs))

    dots = lax.fori_loop(0, cx, dot_plane, tuple(jnp.zeros((8, LANES), F32) for _ in pairs))
    everything = list(grams) + list(dots)
    slot = lax.broadcasted_iota(jnp.int32, (8, LANES), 0)
    quarter = lax.broadcasted_iota(jnp.int32, (8, LANES), 1) // 32
    payload = jnp.zeros((8, LANES), F32)
    for start in range(0, len(everything), 8):
        tile = jnp.zeros((8, LANES), F32)
        for k, part in enumerate(everything[start : start + 8]):
            tile = jnp.where(slot == k, jnp.sum(part, axis=0, keepdims=True), tile)
        tile = tile + pltpu.roll(tile, 64, 1)
        tile = tile + pltpu.roll(tile, 32, 1)
        payload = jnp.where(quarter == start // 8, tile, payload)

    def reduce_over(value, buffer, place, targets, send_sem, recv_sem):
        buffer[place] = value
        sends = []
        for k, target in enumerate(targets):
            sends.append(pltpu.make_async_remote_copy(
                src_ref=buffer.at[place], dst_ref=buffer.at[place],
                send_sem=send_sem.at[k], recv_sem=recv_sem.at[k],
                device_id=target, device_id_type=MESH,
            ))
        for copy in sends:
            copy.start()
        for copy in sends:
            copy.wait()
        total = buffer[0]
        for k in range(1, len(targets) + 1):
            total = total + buffer[k]
        return total

    value = reduce_over(payload, sum_x, gx, greeted[: nx - 1], ax_s, ax_r)
    value = reduce_over(
        value, sum_yz, gy * nz + gz, greeted[nx - 1 : nx - 1 + len(others)], ay_s, ay_r
    )
    value = value * (1.0 / (nx * ny * nz * cx * cy * cz))
    columns = [
        jnp.broadcast_to(
            jnp.sum(jnp.where(quarter == j, value, 0.0), axis=1, keepdims=True), (8, LANES)
        )
        for j in range((len(everything) + 7) // 8)
    ]

    def entry(k):
        return columns[k // 8][k % 8 : k % 8 + 1]

    gram = {pair: entry(k) for k, pair in enumerate(gram_pairs)}
    product = {pair: entry(k + len(gram_pairs)) for k, pair in enumerate(pairs)}
    low, recip = {}, []
    for q in range(nb):
        s = gram[q, q]
        for k in range(q):
            s = s - low[q, k] * low[q, k]
        recip.append(1.0 / jnp.sqrt(s))
        for p in range(q + 1, nb):
            s = gram[p, q]
            for k in range(q):
                s = s - low[p, k] * low[q, k]
            low[p, q] = s * recip[q]
    inv = {}
    for q in range(nb):
        inv[q, q] = recip[q]
        for p in range(q + 1, nb):
            s = low[p, q] * inv[q, q]
            for k in range(q + 1, p):
                s = s + low[p, k] * inv[k, q]
            inv[p, q] = -s * recip[p]

    @pl.loop(0, cx)
    def _(i):
        f = [cur[fslot, b, i + 1, 0:cy, :] for b in range(nb)]
        for p in range(nb):
            total = inv[p, 0] * f[0]
            for q in range(1, p + 1):
                total = total + inv[p, q] * f[q]
            basis_ref[p, i] = total

    left = {}
    for p in range(nb):
        for s in range(nb):
            total = inv[p, 0] * product[0, s]
            for r in range(1, p + 1):
                total = total + inv[p, r] * product[r, s]
            left[p, s] = total
    at_row = lax.broadcasted_iota(jnp.int32, (8, LANES), 0)
    at_lane = lax.broadcasted_iota(jnp.int32, (8, LANES), 1)
    ritz = jnp.zeros((8, LANES), F32)
    for p in range(nb):
        for q in range(nb):
            total = left[p, 0] * inv[q, 0]
            for s in range(1, q + 1):
                total = total + left[p, s] * inv[q, s]
            ritz = jnp.where((at_row == p) & (at_lane == q), total, ritz)
    ritz_ref[...] = ritz[0:nb, 0:nb]


def local(sizes, bands, stencil_coef):
    nx, ny, nz = sizes
    nb, cx, cy, cz = shape = bands.shape
    assert nz == 2 and cz == LANES and cy % 16 == 0 and nb == 4 and nx > 2
    wide, rows, nyz = nb + 1, cy + 8, ny * nz
    up = -(-(cx + 2) // 8) * 8
    dma = pltpu.SemaphoreType.DMA
    return pl.pallas_call(
        functools.partial(kernel, sizes, shape),
        out_shape=(
            jax.ShapeDtypeStruct(shape, F32),
            jax.ShapeDtypeStruct((nb, nb), F32),
        ),
        in_specs=[
            pl.BlockSpec(memory_space=pl.ANY),
            pl.BlockSpec(memory_space=pltpu.SMEM),
        ],
        out_specs=(
            pl.BlockSpec(memory_space=pltpu.VMEM),
            pl.BlockSpec(memory_space=pltpu.VMEM),
        ),
        scratch_shapes=[
            pltpu.VMEM((2, wide, cx + 2, rows, LANES), F32),
            pltpu.VMEM((wide, cx + 2, rows, LANES), F32),
            pltpu.VMEM((wide, cx + 2, rows, LANES), F32),
            pltpu.VMEM((2, cy, LANES), F32),
            pltpu.VMEM((cx, cy // 2, LANES), F32),
            pltpu.VMEM((cx, cy // 2, LANES), F32),
            pltpu.VMEM((NS, 2, wide, cy, LANES), F32),
            pltpu.VMEM((NS, 2, wide, up, LANES), F32),
            pltpu.VMEM((NS, 2, wide, up, LANES), F32),
            pltpu.VMEM((NS, 2, 2, 8, LANES), F32),
            pltpu.VMEM((NS, 2, 2, 8, LANES), F32),
            pltpu.VMEM((nx, 8, LANES), F32),
            pltpu.VMEM((nyz, 8, LANES), F32),
            dma, dma, dma,
            dma((NS, 2)), dma((NS, 2)),
            dma((NS, 2)), dma((NS, 2)),
            dma((NS, 4)), dma((NS, 4)),
            dma((nx - 1,)), dma((nx - 1,)),
            dma((nyz - 1,)), dma((nyz - 1,)),
        ],
        compiler_params=pltpu.CompilerParams(
            collective_id=0, has_side_effects=True, vmem_limit_bytes=40 * 1024 * 1024
        ),
    )(bands, stencil_coef)


def solution(mesh):
    placed = (P(None, "gx", "gy", "gz"), P())
    sizes = (mesh.shape["gx"], mesh.shape["gy"], mesh.shape["gz"])
    return jax.shard_map(
        functools.partial(local, sizes),
        mesh=mesh,
        in_specs=placed,
        out_specs=placed,
        check_vma=False,
    )
```

profile of v0, /device:TPU:0, one launch (start us, length us, event | category | flops | bytes accessed | tf_op | source)
XLA Modules:
  0.0 66.2 jit_solution(4940268843918620659)
XLA Ops:
  0.6 0.0 copy-start
  0.6 1.3 %copy-done = f32[4,12,48,128]{3,2,1,0:T(8,128)S(1)} copy-done((f32[4,12,48,128]{3,2,1,0:T(8,128)S(1)}, f32[4,12,48,128]{3,2,1,0:T(8,128)}, u32[]{:S(2)}) %copy-start) | copy-done | bytes 1179672
  1.9 0.0 copy-start.1
  1.9 0.7 copy-done.1
  2.6 62.1 %shard_map.41 = (f32[4,12,48,128]{3,2,1,0:T(8,128)S(1)}, f32[4,4]{1,0:T(4,128)S(1)}) custom-call(f32[4,12,48,128]{3,2,1,0:T(8,128)S(1)} %copy-done, f32[27]{0:T(128)S(1)} %copy-done.1), custom_call_target="tpu_custom_call" | custom-call | tf_op jit(solution)/shard_map/pallas_call | solution.py:354
  64.6 1.0 %copy.6 = f32[4,12,48,128]{3,2,1,0:T(8,128)} copy(f32[4,12,48,128]{3,2,1,0:T(8,128)S(1)} %get-tuple-element.4) | data formatting | bytes 2359296
  65.6 0.6 copy.7
Async XLA Ops:
  0.6 1.3 %copy-start = (f32[4,12,48,128]{3,2,1,0:T(8,128)S(1)}, f32[4,12,48,128]{3,2,1,0:T(8,128)}, u32[]{:S(2)}) copy-start(f32[4,12,48,128]{3,2,1,0:T(8,128)} %bands_ref.1) | copy-start | bytes 3538948
  1.9 0.7 copy-start.1
where the time goes:
time: 66.4 us; the launch traced here: 66.2 us
  Pallas kernels  62.1 us (94%)
  local copies, waits for them, and re-layouts  3.51 us (5%)
    pallas_call x1, Pallas kernels, local(): pl.pallas_call(functools.partial(kernel, sizes, shape), out_shape=(jax.Sh...  62.1 us
    unnamed x6, local copies, waits for them, and re-layouts  3.51 us

commit v1 on v0

--- a/solution.py
+++ b/solution.py
@@ -28,7 +28,7 @@
 def kernel(
     sizes, shape, bands_ref, coef_ref, basis_ref, ritz_ref,
     cur, zm, zp, kin, packed, arrived, xrecv, ysend, yrecv, csend, crecv,
-    sum_x, sum_yz,
+    sum_x, sum_yz, pick,
     load_sem, zs_sem, zr_sem, xs_sem, xr_sem, ys_sem, yr_sem, cs_sem, cr_sem,
     ax_s, ax_r, ay_s, ay_r,
 ):
@@ -59,6 +59,16 @@
     kin[0] = fy + square(lane + gz * cz, nz * cz)
     strip_z = gz * cz + jnp.where(group < 16, group - 8, group + (cz - 24)) + nz * cz
     kin[1] = fy + square(lax.rem(strip_z, nz * cz), nz * cz)
+
+    take = lax.broadcasted_iota(jnp.int32, (2 * LANES, 2 * LANES), 0)
+    give = lax.broadcasted_iota(jnp.int32, (2 * LANES, 2 * LANES), 1)
+    inside = ((give < LANES) & (take == give - 1)) | (
+        (give >= LANES) & (take < LANES) & (take == give - LANES + 1)
+    )
+    for b in range(nb):
+        before = (give == 0) & (take == LANES + 32 * b + 7)
+        after = (give == 2 * LANES - 1) & (take == LANES + 32 * b + 24)
+        pick[b] = jnp.where(inside | before | after, 1.0, 0.0).astype(jnp.bfloat16)
 
     load.wait()
 
@@ -87,11 +97,57 @@
 
     pl.semaphore_wait(barrier, len(greeted))
 
+    def parts(step):
+        return ((nb, wide), (0, nb)) if step == 0 else ((2, wide), (0, 2))
+
+    def x_sends(step, g):
+        now = step % 2
+        first, last = parts(step)[g]
+        copies = []
+        for i, p in enumerate((1, cx)):
+            copies.append(pltpu.make_async_remote_copy(
+                src_ref=cur.at[now, first:last, p, 0:cy], dst_ref=xrecv.at[step, i, first:last],
+                send_sem=xs_sem.at[step, g, i], recv_sem=xr_sem.at[step, g, i],
+                device_id=dev(2 * i - 1, 0, 0), device_id_type=MESH,
+            ))
+            copies[-1].start()
+        for i, p in enumerate((1, cx)):
+            for j, r in enumerate((0, cy - 1)):
+                for b in range(first, last):
+                    csend[step, g, i, j, b : b + 1, :] = cur[now, b, p, r : r + 1, :]
+                copies.append(pltpu.make_async_remote_copy(
+                    src_ref=csend.at[step, g, i, j], dst_ref=crecv.at[step, g, i, j],
+                    send_sem=cs_sem.at[step, g, 2 * i + j], recv_sem=cr_sem.at[step, g, 2 * i + j],
+                    device_id=dev(2 * i - 1, 2 * j - 1, 0), device_id_type=MESH,
+                ))
+                copies[-1].start()
+        return copies
+
+    def y_sends(step):
+        now = step % 2
+        copies = []
+
+        @pl.loop(0, wide)
+        def _(b):
+            for p in range(1, cx + 1):
+                ysend[step, 0, b, p : p + 1, :] = cur[now, b, p, 0:1, :]
+                ysend[step, 1, b, p : p + 1, :] = cur[now, b, p, cy - 1 : cy, :]
+
+        for j in range(2):
+            copies.append(pltpu.make_async_remote_copy(
+                src_ref=ysend.at[step, j], dst_ref=yrecv.at[step, j],
+                send_sem=ys_sem.at[step, j], recv_sem=yr_sem.at[step, j],
+                device_id=dev(0, 2 * j - 1, 0), device_id_type=MESH,
+            ))
+            copies[-1].start()
+        return copies
+
     z_copy = pltpu.make_async_remote_copy(
         src_ref=packed, dst_ref=arrived, send_sem=zs_sem, recv_sem=zr_sem,
         device_id=dev(0, 0, 1), device_id_type=MESH,
     )
     z_copy.start()
+    x_copies = [None, x_sends(0, 1)]
     z_copy.wait()
 
     @pl.loop(0, cx)
@@ -101,54 +157,28 @@
         full = jnp.concatenate([there, pltpu.roll(there, LANES - 16, 1)], axis=0)
         cur[0, nb, i + 1, 0:cy, :] = jnp.where(outer, full, own)
 
-    def start_sends(step):
-        now = step % 2
-        copies = []
-
-        @pl.loop(0, wide)
-        def _(b):
-            for p in range(1, cx + 1):
-                ysend[step, 0, b, p : p + 1, :] = cur[now, b, p, 0:1, :]
-                ysend[step, 1, b, p : p + 1, :] = cur[now, b, p, cy - 1 : cy, :]
-            for i, p in enumerate((1, cx)):
-                for j, r in enumerate((0, cy - 1)):
-                    csend[step, i, j, pl.ds(b, 1), :] = cur[now, b, p, r : r + 1, :]
-
-        for i, p in enumerate((1, cx)):
-            copies.append(pltpu.make_async_remote_copy(
-                src_ref=cur.at[now, :, p, 0:cy], dst_ref=xrecv.at[step, i],
-                send_sem=xs_sem.at[step, i], recv_sem=xr_sem.at[step, i],
-                device_id=dev(2 * i - 1, 0, 0), device_id_type=MESH,
-            ))
-        for j in range(2):
-            copies.append(pltpu.make_async_remote_copy(
-                src_ref=ysend.at[step, j], dst_ref=yrecv.at[step, j],
-                send_sem=ys_sem.at[step, j], recv_sem=yr_sem.at[step, j],
-                device_id=dev(0, 2 * j - 1, 0), device_id_type=MESH,
-            ))
-        for i in range(2):
-            for j in range(2):
-                copies.append(pltpu.make_async_remote_copy(
-                    src_ref=csend.at[step, i, j], dst_ref=crecv.at[step, i, j],
-                    send_sem=cs_sem.at[step, 2 * i + j], recv_sem=cr_sem.at[step, 2 * i + j],
-                    device_id=dev(2 * i - 1, 2 * j - 1, 0), device_id_type=MESH,
-                ))
-        for copy in copies:
-            copy.start()
-        return copies
-
-    def shift_z(now, plane, first, count):
-        part = pl.ds(first, count)
-        at = lax.broadcasted_iota(jnp.int32, (count, LANES), 1)
-        strip = cur[now, nb, plane, part, :]
-        zm[nb, plane, part, :] = pltpu.roll(strip, 1, 1)
-        zp[nb, plane, part, :] = pltpu.roll(strip, LANES - 1, 1)
-        for b in range(nb):
-            v = cur[now, b, plane, part, :]
-            before = pltpu.roll(strip, (LANES - 32 * b - 7) % LANES, 1)
-            after = pltpu.roll(strip, (LANES - 1 - 32 * b - 24) % LANES, 1)
-            zm[b, plane, part, :] = jnp.where(at == 0, before, pltpu.roll(v, 1, 1))
-            zp[b, plane, part, :] = jnp.where(at == LANES - 1, after, pltpu.roll(v, LANES - 1, 1))
+    def halves(v):
+        high = v.astype(jnp.bfloat16)
+        low = (v - high.astype(F32)).astype(jnp.bfloat16)
+        return jnp.concatenate([high, low], axis=0)
+
+    def shift_z(now, plane, planes, first, count, band=0, end=None):
+        part, which = pl.ds(first, count), pl.ds(plane, planes)
+        m = planes * count
+        strip = cur[now, nb, which, part, :].reshape(m, LANES)
+        end = wide if end is None else end
+        if end == wide:
+            zm[nb, which, part, :] = pltpu.roll(strip, 1, 1).reshape(planes, count, LANES)
+            zp[nb, which, part, :] = pltpu.roll(strip, LANES - 1, 1).reshape(planes, count, LANES)
+        strip = halves(strip)
+        for b in range(band, min(end, nb)):
+            v = halves(cur[now, b, which, part, :].reshape(m, LANES))
+            moved = jnp.dot(
+                jnp.concatenate([v, strip], axis=1), pick[b], preferred_element_type=F32
+            )
+            moved = moved[0:m] + moved[m : 2 * m]
+            zm[b, which, part, :] = moved[:, 0:LANES].reshape(planes, count, LANES)
+            zp[b, which, part, :] = moved[:, LANES:].reshape(planes, count, LANES)
 
     def apply_plane(step, b, plane):
         now, later = step % 2, 1 - step % 2
@@ -184,15 +214,15 @@
             total = total + a[k : k + 8]
         return total
 
-    copies = start_sends(0)
+    x_copies[0] = x_sends(0, 0)
+    y_copies = y_sends(0)
     for step in range(NS):
         now = step % 2
         live = wide if step < DEGREE else nb
-        x_copies, y_copies, c_copies = copies[0:2], copies[2:4], copies[4:8]
-
-        @pl.loop(1, cx + 1)
-        def _(p):
-            shift_z(now, p, 0, cy)
+
+        @pl.loop(0, cx // 4)
+        def _(i):
+            shift_z(now, 4 * i + 1, 4, 0, cy)
 
         if step == DEGREE:
             def gram_plane(p, acc):
@@ -212,36 +242,40 @@
                 cur[now, b, p, cy : cy + 1, :] = yrecv[step, 0, b, p : p + 1, :]
                 cur[now, b, p, rows - 1 : rows, :] = yrecv[step, 1, b, p : p + 1, :]
 
-        @pl.loop(1, cx + 1)
-        def _(p):
-            shift_z(now, p, cy, 8)
+        shift_z(now, 1, cx, cy, 8)
 
         @pl.loop(0, live * (cx - 2))
         def _(t):
             apply_plane(step, t // (cx - 2), lax.rem(t, cx - 2) + 2)
 
-        for copy in x_copies + c_copies:
-            copy.wait_recv()
-
-        @pl.loop(0, wide)
-        def _(b):
-            for i, p in enumerate((cx + 1, 0)):
-                cur[now, b, p, 0:cy, :] = xrecv[step, i, b]
-                cur[now, b, p, cy : cy + 1, :] = crecv[step, i, 0, pl.ds(b, 1), :]
-                cur[now, b, p, rows - 1 : rows, :] = crecv[step, i, 1, pl.ds(b, 1), :]
-
-        for p in (0, cx + 1):
-            shift_z(now, p, 0, rows)
-
-        @pl.loop(0, live)
-        def _(b):
-            apply_plane(step, b, 1)
-            apply_plane(step, b, cx)
-
-        for copy in copies:
+        later_x = []
+        for copy in y_copies + x_copies[0][:2] + x_copies[1][:2]:
             copy.wait_send()
+        for g, (first, last) in enumerate(parts(max(step, 1))):
+            need = x_copies if step == 0 and g == 0 else ([] if step == 0 else [x_copies[g]])
+            for copy in sum(need, []):
+                copy.wait_recv()
+            for b in range(first, last):
+                source = g if step > 0 else (0 if b == nb else 1)
+                for i, p in enumerate((cx + 1, 0)):
+                    cur[now, b, p, 0:cy, :] = xrecv[step, i, b]
+                    cur[now, b, p, cy : cy + 1, :] = crecv[step, source, i, 0, b : b + 1, :]
+                    cur[now, b, p, rows - 1 : rows, :] = crecv[step, source, i, 1, b : b + 1, :]
+            for p in (0, cx + 1):
+                shift_z(now, p, 1, 0, rows, first, last)
+
+            @pl.loop(first, min(last, live))
+            def _(b):
+                apply_plane(step, b, 1)
+                apply_plane(step, b, cx)
+
+            if step < DEGREE:
+                later_x.append(x_sends(step + 1, g))
+        for copy in x_copies[0][2:] + x_copies[1][2:]:
+            copy.wait_send()
+        x_copies = later_x
         if step < DEGREE:
-            copies = start_sends(step + 1)
+            y_copies = y_sends(step + 1)
 
     def dot_plane(p, acc):
         f = [cur[fslot, b, p + 1, 0:cy, :] for b in range(nb)]
@@ -347,7 +381,7 @@
 def local(sizes, bands, stencil_coef):
     nx, ny, nz = sizes
     nb, cx, cy, cz = shape = bands.shape
-    assert nz == 2 and cz == LANES and cy % 16 == 0 and nb == 4 and nx > 2
+    assert nz == 2 and cz == LANES and cy % 16 == 0 and nb == 4 and nx > 2 and cx % 4 == 0
     wide, rows, nyz = nb + 1, cy + 8, ny * nz
     up = -(-(cx + 2) // 8) * 8
     dma = pltpu.SemaphoreType.DMA
@@ -375,14 +409,15 @@
             pltpu.VMEM((NS, 2, wide, cy, LANES), F32),
             pltpu.VMEM((NS, 2, wide, up, LANES), F32),
             pltpu.VMEM((NS, 2, wide, up, LANES), F32),
-            pltpu.VMEM((NS, 2, 2, 8, LANES), F32),
-            pltpu.VMEM((NS, 2, 2, 8, LANES), F32),
+            pltpu.VMEM((NS, 2, 2, 2, 8, LANES), F32),
+            pltpu.VMEM((NS, 2, 2, 2, 8, LANES), F32),
             pltpu.VMEM((nx, 8, LANES), F32),
             pltpu.VMEM((nyz, 8, LANES), F32),
+            pltpu.VMEM((nb, 2 * LANES, 2 * LANES), jnp.bfloat16),
             dma, dma, dma,
+            dma((NS, 2, 2)), dma((NS, 2, 2)),
             dma((NS, 2)), dma((NS, 2)),
-            dma((NS, 2)), dma((NS, 2)),
-            dma((NS, 4)), dma((NS, 4)),
+            dma((NS, 2, 4)), dma((NS, 2, 4)),
             dma((nx - 1,)), dma((nx - 1,)),
             dma((nyz - 1,)), dma((nyz - 1,)),
         ],

time: 66.4 us -> 61.9 us (0.932)
  Pallas kernels: 62.1 us -> 57.6 us
    pallas_call x1, Pallas kernels: 62.1 us -> 57.6 us  [local(): pl.pallas_call(functools.partial(kernel, sizes, shape), out_shape=(jax.Sh...]
where the time goes in v1:
time: 61.9 us; the launch traced here: 61.7 us
  Pallas kernels  57.6 us (93%)
  local copies, waits for them, and re-layouts  3.51 us (6%)
  between operations  0.65 us (1%)
    pallas_call x1, Pallas kernels, local(): pl.pallas_call(functools.partial(kernel, sizes, shape), out_shape=(jax.Sh...  57.6 us
    unnamed x6, local copies, waits for them, and re-layouts  3.51 us

profile of v1, /device:TPU:0, one launch (start us, length us, event | category | flops | bytes accessed | tf_op | source)
XLA Modules:
  0.0 61.7 jit_solution(5291072436395435497)
XLA Ops:
  0.6 0.0 copy-start
  0.6 1.3 %copy-done = f32[4,12,48,128]{3,2,1,0:T(8,128)S(1)} copy-done((f32[4,12,48,128]{3,2,1,0:T(8,128)S(1)}, f32[4,12,48,128]{3,2,1,0:T(8,128)}, u32[]{:S(2)}) %copy-start) | copy-done | bytes 1179672
  1.9 0.0 copy-start.1
  1.9 0.7 %copy-done.1 = f32[27]{0:T(128)S(1)} copy-done((f32[27]{0:T(128)S(1)}, f32[27]{0:T(128)}, u32[]{:S(2)}) %copy-start.1) | copy-done | bytes 132
  2.6 57.6 %shard_map.41 = (f32[4,12,48,128]{3,2,1,0:T(8,128)S(1)}, f32[4,4]{1,0:T(4,128)S(1)}) custom-call(f32[4,12,48,128]{3,2,1,0:T(8,128)S(1)} %copy-done, f32[27]{0:T(128)S(1)} %copy-done.1), custom_call_target="tpu_custom_call" | custom-call | tf_op jit(solution)/shard_map/pallas_call | solution.py:388
  60.1 1.0 %copy.6 = f32[4,12,48,128]{3,2,1,0:T(8,128)} copy(f32[4,12,48,128]{3,2,1,0:T(8,128)S(1)} %get-tuple-element.4) | data formatting | bytes 2359296
  61.2 0.6 copy.7
Async XLA Ops:
  0.6 1.3 %copy-start = (f32[4,12,48,128]{3,2,1,0:T(8,128)S(1)}, f32[4,12,48,128]{3,2,1,0:T(8,128)}, u32[]{:S(2)}) copy-start(f32[4,12,48,128]{3,2,1,0:T(8,128)} %bands_ref.1) | copy-start | bytes 3538948
  1.9 0.7 %copy-start.1 = (f32[27]{0:T(128)S(1)}, f32[27]{0:T(128)}, u32[]{:S(2)}) copy-start(f32[27]{0:T(128)} %coef_ref.1) | copy-start | bytes 328

commit v2 on v1

--- a/solution.py
+++ b/solution.py
@@ -28,7 +28,7 @@
 def kernel(
     sizes, shape, bands_ref, coef_ref, basis_ref, ritz_ref,
     cur, zm, zp, kin, packed, arrived, xrecv, ysend, yrecv, csend, crecv,
-    sum_x, sum_yz, pick,
+    sum_x, sum_yz, pick, edge_coef,
     load_sem, zs_sem, zr_sem, xs_sem, xr_sem, ys_sem, yr_sem, cs_sem, cr_sem,
     ax_s, ax_r, ay_s, ay_r,
 ):
@@ -69,6 +69,13 @@
         before = (give == 0) & (take == LANES + 32 * b + 7)
         after = (give == 2 * LANES - 1) & (take == LANES + 32 * b + 24)
         pick[b] = jnp.where(inside | before | after, 1.0, 0.0).astype(jnp.bfloat16)
+
+    tile_row = lax.broadcasted_iota(jnp.int32, (8, LANES), 0)
+    for x in range(3):
+        for z in range(3):
+            edge_coef[3 * x + z] = jnp.where(
+                tile_row < 4, coef_ref[9 * x + 6 + z], coef_ref[9 * x + z]
+            )
 
     load.wait()
 
@@ -123,11 +130,12 @@
                 copies[-1].start()
         return copies
 
-    def y_sends(step):
+    def y_sends(step, g):
         now = step % 2
+        first, last = parts(step)[g]
         copies = []
 
-        @pl.loop(0, wide)
+        @pl.loop(first, last)
         def _(b):
             for p in range(1, cx + 1):
                 ysend[step, 0, b, p : p + 1, :] = cur[now, b, p, 0:1, :]
@@ -135,8 +143,8 @@
 
         for j in range(2):
             copies.append(pltpu.make_async_remote_copy(
-                src_ref=ysend.at[step, j], dst_ref=yrecv.at[step, j],
-                send_sem=ys_sem.at[step, j], recv_sem=yr_sem.at[step, j],
+                src_ref=ysend.at[step, j, first:last], dst_ref=yrecv.at[step, j, first:last],
+                send_sem=ys_sem.at[step, g, j], recv_sem=yr_sem.at[step, g, j],
                 device_id=dev(0, 2 * j - 1, 0), device_id_type=MESH,
             ))
             copies[-1].start()
@@ -148,6 +156,7 @@
     )
     z_copy.start()
     x_copies = [None, x_sends(0, 1)]
+    y_copies = [None, y_sends(0, 1)]
     z_copy.wait()
 
     @pl.loop(0, cx)
@@ -189,10 +198,16 @@
             for x in range(3):
                 for z in range(3):
                     c = coef_ref[9 * x + 3 * y + z]
-                    span = pl.ds(0, cy) if y == 1 else pl.ds(0, rows)
-                    term = c * fields[z][b, plane + (x - 1), span, :]
+                    term = c * fields[z][b, plane + (x - 1), 0:cy, :]
                     total = term if total is None else total + term
             sums.append(total)
+        edge = None
+        for x in range(3):
+            for z in range(3):
+                term = edge_coef[3 * x + z] * fields[z][b, plane + (x - 1), cy:rows, :]
+                edge = term if edge is None else edge + term
+        sums[0] = jnp.concatenate([sums[0], edge], axis=0)
+        sums[2] = jnp.concatenate([sums[2], edge], axis=0)
         v = cur[now, b, plane, 0:cy, :]
         scale = 1.0 / HALF if step == 0 else (2.0 / HALF if step < DEGREE else 1.0)
         fx = square(gx * cx + plane - 1, nx * cx)
@@ -215,7 +230,7 @@
         return total
 
     x_copies[0] = x_sends(0, 0)
-    y_copies = y_sends(0)
+    y_copies[0] = y_sends(0, 0)
     for step in range(NS):
         now = step % 2
         live = wide if step < DEGREE else nb
@@ -233,23 +248,25 @@
                 0, cx, gram_plane, tuple(jnp.zeros((8, LANES), F32) for _ in gram_pairs)
             )
 
-        for copy in y_copies:
-            copy.wait_recv()
-
-        @pl.loop(0, wide)
-        def _(b):
-            for p in range(1, cx + 1):
-                cur[now, b, p, cy : cy + 1, :] = yrecv[step, 0, b, p : p + 1, :]
-                cur[now, b, p, rows - 1 : rows, :] = yrecv[step, 1, b, p : p + 1, :]
-
-        shift_z(now, 1, cx, cy, 8)
-
-        @pl.loop(0, live * (cx - 2))
-        def _(t):
-            apply_plane(step, t // (cx - 2), lax.rem(t, cx - 2) + 2)
-
-        later_x = []
-        for copy in y_copies + x_copies[0][:2] + x_copies[1][:2]:
+        for g, (first, last) in enumerate(parts(max(step, 1))):
+            need = [y_copies[g]] if step > 0 else (y_copies if g == 0 else [])
+            for copy in sum(need, []):
+                copy.wait_recv()
+
+            @pl.loop(first, last)
+            def _(b):
+                for p in range(1, cx + 1):
+                    cur[now, b, p, cy : cy + 1, :] = yrecv[step, 0, b, p : p + 1, :]
+                    cur[now, b, p, rows - 1 : rows, :] = yrecv[step, 1, b, p : p + 1, :]
+
+            shift_z(now, 1, cx, cy, 8, first, last)
+
+            @pl.loop(0, (min(last, live) - first) * (cx - 2))
+            def _(t):
+                apply_plane(step, first + t // (cx - 2), lax.rem(t, cx - 2) + 2)
+
+        later_x, later_y = [], []
+        for copy in y_copies[0] + y_copies[1] + x_copies[0][:2] + x_copies[1][:2]:
             copy.wait_send()
         for g, (first, last) in enumerate(parts(max(step, 1))):
             need = x_copies if step == 0 and g == 0 else ([] if step == 0 else [x_copies[g]])
@@ -271,11 +288,10 @@
 
             if step < DEGREE:
                 later_x.append(x_sends(step + 1, g))
+                later_y.append(y_sends(step + 1, g))
         for copy in x_copies[0][2:] + x_copies[1][2:]:
             copy.wait_send()
-        x_copies = later_x
-        if step < DEGREE:
-            y_copies = y_sends(step + 1)
+        x_copies, y_copies = later_x, later_y
 
     def dot_plane(p, acc):
         f = [cur[fslot, b, p + 1, 0:cy, :] for b in range(nb)]
@@ -392,7 +408,7 @@
             jax.ShapeDtypeStruct((nb, nb), F32),
         ),
         in_specs=[
-            pl.BlockSpec(memory_space=pl.ANY),
+            pl.BlockSpec(memory_space=pltpu.HBM),
             pl.BlockSpec(memory_space=pltpu.SMEM),
         ],
         out_specs=(
@@ -414,9 +430,10 @@
             pltpu.VMEM((nx, 8, LANES), F32),
             pltpu.VMEM((nyz, 8, LANES), F32),
             pltpu.VMEM((nb, 2 * LANES, 2 * LANES), jnp.bfloat16),
+            pltpu.VMEM((9, 8, LANES), F32),
             dma, dma, dma,
             dma((NS, 2, 2)), dma((NS, 2, 2)),
-            dma((NS, 2)), dma((NS, 2)),
+            dma((NS, 2, 2)), dma((NS, 2, 2)),
             dma((NS, 2, 4)), dma((NS, 2, 4)),
             dma((nx - 1,)), dma((nx - 1,)),
             dma((nyz - 1,)), dma((nyz - 1,)),

time: 61.9 us -> 61.9 us (level)
  no operation moved by 1% of the time
where the time goes in v2:
time: 61.9 us; the launch traced here: 61.8 us
  Pallas kernels  57.6 us (93%)
  local copies, waits for them, and re-layouts  3.51 us (6%)
  between operations  0.65 us (1%)
    pallas_call x1, Pallas kernels, local(): pl.pallas_call(functools.partial(kernel, sizes, shape), out_shape=(jax.Sh...  57.6 us
    unnamed x6, local copies, waits for them, and re-layouts  3.51 us

profile of v2, /device:TPU:0, one launch (start us, length us, event | category | flops | bytes accessed | tf_op | source)
XLA Modules:
  0.0 61.8 jit_solution(7082526019758702366)
XLA Ops:
  0.6 0.0 copy-start
  0.6 1.3 %copy-done = f32[4,12,48,128]{3,2,1,0:T(8,128)S(1)} copy-done((f32[4,12,48,128]{3,2,1,0:T(8,128)S(1)}, f32[4,12,48,128]{3,2,1,0:T(8,128)}, u32[]{:S(2)}) %copy-start) | copy-done | bytes 1179672
  1.9 0.0 copy-start.1
  1.9 0.7 %copy-done.1 = f32[27]{0:T(128)S(1)} copy-done((f32[27]{0:T(128)S(1)}, f32[27]{0:T(128)}, u32[]{:S(2)}) %copy-start.1) | copy-done | bytes 132
  2.6 57.6 %shard_map.41 = (f32[4,12,48,128]{3,2,1,0:T(8,128)S(1)}, f32[4,4]{1,0:T(4,128)S(1)}) custom-call(f32[4,12,48,128]{3,2,1,0:T(8,128)S(1)} %copy-done, f32[27]{0:T(128)S(1)} %copy-done.1), custom_call_target="tpu_custom_call" | custom-call | tf_op jit(solution)/shard_map/pallas_call | solution.py:404
  60.2 1.0 %copy.6 = f32[4,12,48,128]{3,2,1,0:T(8,128)} copy(f32[4,12,48,128]{3,2,1,0:T(8,128)S(1)} %get-tuple-element.4) | data formatting | bytes 2359296
  61.2 0.6 copy.7
Async XLA Ops:
  0.6 1.3 %copy-start = (f32[4,12,48,128]{3,2,1,0:T(8,128)S(1)}, f32[4,12,48,128]{3,2,1,0:T(8,128)}, u32[]{:S(2)}) copy-start(f32[4,12,48,128]{3,2,1,0:T(8,128)} %bands_ref.1) | copy-start | bytes 3538948
  1.9 0.7 %copy-start.1 = (f32[27]{0:T(128)S(1)}, f32[27]{0:T(128)}, u32[]{:S(2)}) copy-start(f32[27]{0:T(128)} %coef_ref.1) | copy-start | bytes 328

commit v3 on v2

--- a/solution.py
+++ b/solution.py
@@ -439,7 +439,7 @@
             dma((nyz - 1,)), dma((nyz - 1,)),
         ],
         compiler_params=pltpu.CompilerParams(
-            collective_id=0, has_side_effects=True, vmem_limit_bytes=40 * 1024 * 1024
+            collective_id=0, has_side_effects=True, vmem_limit_bytes=60 * 1024 * 1024
         ),
     )(bands, stencil_coef)
 

time: 61.9 us -> 63.3 us (1.023)
  Pallas kernels: 57.6 us -> 59.6 us
    pallas_call x1, Pallas kernels: 57.6 us -> 59.6 us  [local(): pl.pallas_call(functools.partial(kernel, sizes, shape), out_shape=(jax.Sh...]
    unnamed x6 -> x4, local copies, waits for them, and re-layouts: 3.51 us -> 2.94 us
where the time goes in v3:
time: 63.3 us; the launch traced here: 63.2 us
  Pallas kernels  59.6 us (94%)
  local copies, waits for them, and re-layouts  2.94 us (5%)
  between operations  0.65 us (1%)
    pallas_call x1, Pallas kernels, local(): pl.pallas_call(functools.partial(kernel, sizes, shape), out_shape=(jax.Sh...  59.6 us
    unnamed x4, local copies, waits for them, and re-layouts  2.94 us

profile of v3, /device:TPU:0, one launch (start us, length us, event | category | flops | bytes accessed | tf_op | source)
XLA Modules:
  0.0 63.2 jit_solution(6082221552935494646)
XLA Ops:
  0.6 59.6 %shard_map.41 = (f32[4,12,48,128]{3,2,1,0:T(8,128)}, f32[4,4]{1,0:T(4,128)}) custom-call(f32[4,12,48,128]{3,2,1,0:T(8,128)} %bands_ref.1, f32[27]{0:T(128)} %coef_ref.1), custom_call_target="tpu_custom_call" | custom-call | tf_op jit(solution)/shard_map/pallas_call | solution.py:404
  60.2 0.0 copy-start
  60.2 2.4 %copy.6 = f32[4,12,48,128]{3,2,1,0:T(8,128)} copy(f32[4,12,48,128]{3,2,1,0:T(8,128)} %get-tuple-element.4) | data formatting | bytes 2359296
  62.6 0.0 copy-done
  62.6 0.6 copy.7
Async XLA Ops:
  60.2 2.4 %copy-start = (f32[4,4]{1,0:T(4,128)S(1)}, f32[4,4]{1,0:T(4,128)}, u32[]{:S(2)}) copy-start(f32[4,4]{1,0:T(4,128)} %get-tuple-element.5) | copy-start | bytes 196
